TPU v7x, 32 devices: a whole 2x2x4 slice. The times are simulated.
32 devices in a mesh: grp: 2 (over y), gx: 16 (over z, x, core).
Axes of the slice: x: 2, y: 2, z: 4, core: 2. Of those that a mesh axis runs over, the one named last changes fastest.
Arguments:
- features: bfloat16 [128, 32, 64, 128], P('grp', 'gx'), parts along dimension 0, may hold values from -6 to 6
- cotangent: bfloat16 [128, 32, 64, 128], P('grp', 'gx'), parts along dimension 0, may hold values from -6 to 6
- spectral_weight: bfloat16 [16384, 64, 128], P('gx'), may hold values from -0.5 to 0.5
- channel_weight: bfloat16 [64, 64], replicated, may hold values from -0.75 to 0.75
- channel_bias: float32 [64], replicated, may hold values from -3 to 3
Outputs:
- activated: bfloat16 [128, 32, 64, 128], P('grp', 'gx'), parts along dimension 0
- feature_grad: bfloat16 [128, 32, 64, 128], P('grp', 'gx'), parts along dimension 0
- spectral_grad: bfloat16 [32768, 64, 128], P(('grp', 'gx')), parts along dimension 0
There are 2 independent parts, one for each index of `grp`. A program takes and returns all parts, laid end to end along the dimension named above; an argument that names none is the same for every part. Nothing has to cross between parts.
All inputs are finite; a program needn't handle non-finite values.
Results may differ from a plain program's by a relative error of at most 0.018.
Values may be sent and summed in bfloat16 or wider, within the bound.
A program may use at most 192 MiB of HBM per device.

v0:
```python
import math
import jax
import jax.numpy as jnp
from jax import lax
from jax.sharding import PartitionSpec as P

MX = 32
MY = 32
MZ = 16
SQRT_TWO_PI = math.sqrt(2.0 / math.pi)
CUBIC_COEF = 0.044715


def freq_index(retained, length):
    ladder = jnp.arange(retained, dtype=jnp.int32)
    return jnp.where(ladder < retained // 2, ladder, length - retained + ladder)


def cos_sin(wavenum, length):
    points = jnp.arange(length, dtype=jnp.int32)
    angles = (wavenum[:, None] * points[None, :] % length).astype(jnp.float32) * (
        2.0 * math.pi / length
    )
    return (jnp.cos(angles), jnp.sin(angles))


def analysis_pair(wavenum, length):
    cosine, sine_wave = cos_sin(wavenum, length)
    cosine, sine_wave = (cosine.T, sine_wave.T)
    return jnp.stack(
        [jnp.stack([cosine, -sine_wave], 1), jnp.stack([sine_wave, cosine], 1)], 1
    ).astype(jnp.bfloat16)


def synthesis_pair(wavenum, length):
    cosine, sine_wave = cos_sin(wavenum, length)
    return jnp.stack(
        [jnp.stack([cosine, sine_wave], 1), jnp.stack([-sine_wave, cosine], 1)], 1
    ).astype(jnp.bfloat16)


def depth_table(retained, length):
    cosine, sine_wave = cos_sin(jnp.arange(retained, dtype=jnp.int32), length)
    return jnp.concatenate([cosine, -sine_wave], 0).astype(jnp.bfloat16)


def gelu_parts(inputs):
    cubed_in = inputs * inputs * inputs
    tangent = jnp.tanh(SQRT_TWO_PI * (inputs + CUBIC_COEF * cubed_in))
    output = 0.5 * inputs * (1.0 + tangent)
    derivative = 0.5 * (1.0 + tangent) + 0.5 * inputs * (1.0 - tangent * tangent) * SQRT_TWO_PI * (
        1.0 + 3.0 * CUBIC_COEF * inputs * inputs
    )
    return (output, derivative)


def mode_product(coeffs, weights, channels):
    stacked = coeffs.reshape(coeffs.shape[0], 2, channels)
    halves = jnp.einsum("mac,mcj->amj", stacked, weights, preferred_element_type=jnp.float32)
    real_out = halves[0, :, :channels] - halves[1, :, channels:]
    imag_out = halves[0, :, channels:] + halves[1, :, :channels]
    return jnp.concatenate([real_out, imag_out], 1).astype(jnp.bfloat16)


def mode_grads(coeffs, weights, grad_modes, channels, weight_scale, input_scale):
    number = coeffs.shape[0]
    stacked = coeffs.reshape(number, 2, channels)
    grad_pairs = grad_modes.reshape(number, 2, channels)
    real_w = jnp.einsum("mac,mao->mco", stacked, grad_pairs, preferred_element_type=jnp.float32)
    imag_w = jnp.einsum(
        "mc,mo->mco", stacked[:, 0], grad_pairs[:, 1], preferred_element_type=jnp.float32
    ) - jnp.einsum(
        "mc,mo->mco", stacked[:, 1], grad_pairs[:, 0], preferred_element_type=jnp.float32
    )
    weight_grad = (jnp.concatenate([real_w, imag_w], 2) * weight_scale).astype(jnp.bfloat16)
    straight = jnp.concatenate([grad_pairs[:, 0], grad_pairs[:, 1]], 1)
    rotated = jnp.concatenate([grad_pairs[:, 1], -grad_pairs[:, 0]], 1)
    real_x = jnp.einsum("mcj,mj->mc", weights, straight, preferred_element_type=jnp.float32)
    imag_x = jnp.einsum("mcj,mj->mc", weights, rotated, preferred_element_type=jnp.float32)
    input_grad = (jnp.concatenate([real_x, imag_x], 1) * input_scale).astype(jnp.bfloat16)
    return (weight_grad, input_grad)


def body(features, cotangent, spectral_weight, channel_weight, channel_bias):
    channels, planes, lines, depth_len = features.shape
    devices = lax.axis_size("gx")
    all_planes = planes * devices
    first_plane = lax.axis_index("gx") * planes
    owned_modes = spectral_weight.shape[0]
    wave_pairs = MY * MZ
    forward_scale = 1.0 / math.sqrt(all_planes * lines * depth_len)
    inverse_scale = 1.0 / math.sqrt(MX * wave_pairs)
    weight_scale = math.sqrt(MX * wave_pairs / (all_planes * lines * depth_len))
    depth_basis = depth_table(MZ, depth_len)
    across_y = analysis_pair(freq_index(MY, lines), lines)
    back_y = synthesis_pair(freq_index(MY, lines), lines)
    across_full = analysis_pair(freq_index(MX, all_planes), all_planes)
    back_full = synthesis_pair(freq_index(MX, all_planes), all_planes)
    across_local = lax.dynamic_slice_in_dim(across_full, first_plane, planes, 0)
    back_local = lax.dynamic_slice_in_dim(back_full, first_plane, planes, 3)
    depth_part = jnp.dot(features, depth_basis.T, preferred_element_type=jnp.float32).astype(
        jnp.bfloat16
    )
    plane_part = (
        jnp.einsum(
            "cxyaz,yabk->cxbkz",
            depth_part.reshape(channels, planes, lines, 2, MZ),
            across_y,
            preferred_element_type=jnp.float32,
        )
        .astype(jnp.bfloat16)
        .reshape(channels, planes, 2, wave_pairs)
    )
    section = plane_part
    mode_sums = lax.psum_scatter(
        jnp.einsum(
            "cxaq,xabk->qkbc", section, across_local, preferred_element_type=jnp.float32
        ).reshape(lax.axis_size("gx") * owned_modes, 2 * channels),
        "gx",
        scatter_dimension=0,
        tiled=True,
    )
    coeffs = (mode_sums * forward_scale).astype(jnp.bfloat16)
    spectral = mode_product(coeffs, spectral_weight, channels)
    every_mode = lax.all_gather(spectral, "gx", axis=0, tiled=True)
    planes_back = jnp.einsum(
        "qkao,kabx->oxbq",
        every_mode.reshape(wave_pairs, MX, 2, channels),
        back_local,
        preferred_element_type=jnp.float32,
    ).astype(jnp.bfloat16)
    lines_back = (
        jnp.einsum(
            "oxakz,kaby->oxybz",
            planes_back.reshape(channels, planes, 2, MY, MZ),
            back_y,
            preferred_element_type=jnp.float32,
        )
        .astype(jnp.bfloat16)
        .reshape(channels, planes, lines, 2 * MZ)
    )
    spectral_term = (
        jnp.dot(lines_back, depth_basis, preferred_element_type=jnp.float32) * inverse_scale
    )
    pointwise = jnp.einsum(
        "oc,cxyz->oxyz", channel_weight, features, preferred_element_type=jnp.float32
    )
    hidden = spectral_term + pointwise + channel_bias[:, None, None, None]
    activated, derivative = gelu_parts(hidden)
    upstream = (cotangent.astype(jnp.float32) * derivative).astype(jnp.bfloat16)
    lines_grad = (
        jnp.dot(upstream, depth_basis.T, preferred_element_type=jnp.float32) * inverse_scale
    ).astype(jnp.bfloat16)
    rows_grad = (
        jnp.einsum(
            "oxybz,kaby->oxakz",
            lines_grad.reshape(channels, planes, lines, 2, MZ),
            back_y,
            preferred_element_type=jnp.float32,
        )
        .astype(jnp.bfloat16)
        .reshape(channels, planes, 2, wave_pairs)
    )
    section = rows_grad
    grad_sums = lax.psum_scatter(
        jnp.einsum(
            "oxbq,kabx->qkao", section, back_local, preferred_element_type=jnp.float32
        ).reshape(lax.axis_size("gx") * owned_modes, 2 * channels),
        "gx",
        scatter_dimension=0,
        tiled=True,
    )
    grad_modes = grad_sums.astype(jnp.bfloat16)
    spectral_grad, coeff_grad = mode_grads(
        coeffs, spectral_weight, grad_modes, channels, weight_scale, forward_scale
    )
    every_grad = lax.all_gather(coeff_grad, "gx", axis=0, tiled=True)
    plane_grad = jnp.einsum(
        "qkbc,xabk->cxaq",
        every_grad.reshape(wave_pairs, MX, 2, channels),
        across_local,
        preferred_element_type=jnp.float32,
    ).astype(jnp.bfloat16)
    depth_grad = (
        jnp.einsum(
            "cxbkz,yabk->cxyaz",
            plane_grad.reshape(channels, planes, 2, MY, MZ),
            across_y,
            preferred_element_type=jnp.float32,
        )
        .astype(jnp.bfloat16)
        .reshape(channels, planes, lines, 2 * MZ)
    )
    channel_back = jnp.einsum(
        "oc,oxyz->cxyz", channel_weight, upstream, preferred_element_type=jnp.float32
    )
    feature_grad = (
        jnp.dot(depth_grad, depth_basis, preferred_element_type=jnp.float32) + channel_back
    ).astype(jnp.bfloat16)
    return (activated.astype(jnp.bfloat16), feature_grad, spectral_grad)


def solution(mesh):
    in_specs = (
        P("grp", "gx", None, None),
        P("grp", "gx", None, None),
        P("gx", None, None),
        P(),
        P(),
    )
    out_specs = (
        P("grp", "gx", None, None),
        P("grp", "gx", None, None),
        P(("grp", "gx"), None, None),
    )
    return jax.shard_map(body, mesh=mesh, in_specs=in_specs, out_specs=out_specs, check_vma=False)
```

profile of v0, /device:TPU:0, one launch (start us, length us, event | category | flops | bytes accessed | tf_op | source)
XLA Modules:
  0.0 581.4 jit_solution(1618239725951916792)
XLA Ops:
  8.8 2.1 convolution_convert_fusion
  12.7 4.8 convolution_bitcast_fusion.1
  17.5 16.1 %copy.116 = f32[512,32,2,64]{3,2,1,0:T(2,128)} copy(f32[512,32,2,64]{0,1,3,2:T(8,128)} %convolution_bitcast_fusion.1) | data formatting | bytes 16777216 | tf_op jit(solution)/shard_map/cxaq,xabk->qkbc/transpose | solution.py:116
  33.6 16.4 %reshape.402 = f32[16384,128]{1,0:T(8,128)} reshape(f32[512,32,2,64]{3,2,1,0:T(2,128)} %copy.116) | data formatting | bytes 16777216 | tf_op jit(solution)/shard_map/reshape | solution.py:118
  50.1 107.4 %reduce-scatter.3.cloned.1.call-done = f32[1024,128]{1,0:T(8,128)} async-done(((f32[16384,128]{1,0:T(8,128)}), f32[1024,128]{1,0:T(8,128)}) %reduce-scatter.3.cloned.1.call-update) | async-done | bytes 524304 | tf_op jit(solution)/shard_map/reduce_scatter | solution.py:115
  159.2 8.9 %fusion.114 = f32[1024,2,128]{2,1,0:T(2,128)} fusion(bf16[1024,2,64]{2,1,0:T(2,128)(2,1)S(1)} %copy.118, bf16[1024,64,128]{2,1,0:T(8,128)(2,1)} %param.7), kind=kOutput, calls=%fused_computation.163 | convolution fusion | flops 33554432 | bytes 18087936 | tf_op jit(solution)/shard_map/mac,mcj->amj/dot_general | solution.py:59
  168.0 2.3 copy.119
  173.1 3.6 fusion.18
  176.7 46.1 %all-gather.3.cloned.1.call-done = bf16[16384,128]{0,1:T(8,128)(2,1)} async-done(((bf16[1024,128]{0,1:T(8,128)(2,1)}), bf16[16384,128]{0,1:T(8,128)(2,1)}) %all-gather.3.cloned.1.call-update) | async-done | bytes 4194320 | tf_op jit(solution)/shard_map/all_gather | solution.py:125
  222.8 6.4 %copy.120 = bf16[16384,128]{1,0:T(8,128)(2,1)} copy(bf16[16384,128]{0,1:T(8,128)(2,1)} %all-gather.3.cloned.1.call-done) | data formatting | bytes 8388608 | tf_op jit(solution)/shard_map/all_gather | solution.py:125
  229.2 14.7 %reshape.404 = bf16[512,32,2,64]{3,2,1,0:T(2,128)(2,1)} reshape(bf16[16384,128]{1,0:T(8,128)(2,1)} %copy.120) | data formatting | bytes 8388608 | tf_op jit(solution)/shard_map/reshape | solution.py:128
  243.9 15.3 %copy.122 = bf16[512,32,2,64]{0,1,2,3:T(8,128)(2,1)} copy(bf16[512,32,2,64]{3,2,1,0:T(2,128)(2,1)} %reshape.404) | data formatting | bytes 8388608 | tf_op jit(solution)/shard_map/reshape | solution.py:128
  259.2 3.0 fusion.41
  263.0 2.5 copy.125
  265.4 11.8 %fusion.9 = (bf16[64,2,64,128]{3,2,1,0:T(8,128)(2,1)S(1)}, bf16[64,2,64,128]{3,2,1,0:T(8,128)(2,1)}) fusion(bf16[64,2,64,128]{3,2,1,0:T(8,128)(2,1)} %param.6, f32[64]{0:T(128)S(1)} %copy-done.9, f32[64,2,64,128]{3,0,2,1:T(8,128)} %fusion.18, bf16[64,2,64,32]{2,3,1,0:T(8,128)(2,1)} %bitcast.244, bf16[16,128]{1,0:T(8,128)(2,1)S(1)} %get-tuple-element.31, ...), kind=kOutput, calls=%fused_computation.13 | convolution fusion | flops 93339648 | bytes 11018496 | tf_op jit(solution)/shard_map/dot_general | solution.py:143
  277.2 2.1 multiply_convert_fusion.1
  283.0 4.6 convolution_bitcast_fusion
  287.6 16.1 %copy.133 = f32[512,32,2,64]{3,2,1,0:T(2,128)} copy(f32[512,32,2,64]{0,1,3,2:T(8,128)} %convolution_bitcast_fusion) | data formatting | bytes 16777216 | tf_op jit(solution)/shard_map/oxbq,kabx->qkao/transpose | solution.py:166
  303.8 16.4 %reshape.409 = f32[16384,128]{1,0:T(8,128)} reshape(f32[512,32,2,64]{3,2,1,0:T(2,128)} %copy.133) | data formatting | bytes 16777216 | tf_op jit(solution)/shard_map/reshape | solution.py:168
  320.3 103.3 %reduce-scatter.5.cloned.1.call-done = f32[1024,128]{1,0:T(8,128)} async-done(((f32[16384,128]{1,0:T(8,128)}), f32[1024,128]{1,0:T(8,128)}) %reduce-scatter.5.cloned.1.call-update) | async-done | bytes 524304 | tf_op jit(solution)/shard_map/reduce_scatter | solution.py:165
  426.4 2.1 copy.164
  428.6 13.0 %fusion.115 = f32[1024,1,64]{2,1,0:T(1,128)} fusion(bf16[1024,128,1]{1,2,0:T(2,128)(2,1)} %copy.164, bf16[1024,64,128]{2,1,0:T(8,128)(2,1)} %param.7), kind=kOutput, calls=%fused_computation.164 | convolution fusion | flops 16777216 | bytes 17301504 | tf_op jit(solution)/shard_map/mcj,mj->mc/dot_general | solution.py:78
  442.7 12.4 %fusion.116 = f32[1024,1,64]{2,1,0:T(1,128)S(1)} fusion(bf16[1024,128,1]{1,2,0:T(2,128)(2,1)} %copy.166, bf16[1024,64,128]{2,1,0:T(8,128)(2,1)} %param.7), kind=kOutput, calls=%fused_computation.165 | convolution fusion | flops 16777216 | bytes 17301504 | tf_op jit(solution)/shard_map/mcj,mj->mc/dot_general | solution.py:79
  460.0 3.7 fusion.16
  466.4 12.4 %fusion.117 = f32[1024,64,64]{2,1,0:T(8,128)} fusion(bf16[1024,2,64]{2,1,0:T(2,128)(2,1)S(1)} %copy.118, bf16[1024,2,64]{2,1,0:T(2,128)(2,1)S(1)} %copy.145), kind=kOutput, calls=%fused_computation.166 | convolution fusion | flops 16777216 | bytes 17301504 | tf_op jit(solution)/shard_map/mac,mao->mco/dot_general | solution.py:69
  478.8 22.8 %multiply_subtract_fusion = f32[1024,64,64]{2,1,0:T(8,128)} fusion(f32[1024,64]{1,0:T(8,128)S(1)} %copy.149, f32[1024,64]{1,0:T(8,128)S(1)} %copy-done.2, f32[1024,64]{1,0:T(8,128)S(1)} %copy.147, f32[1024,64]{1,0:T(8,128)S(1)} %copy.146), kind=kLoop, calls=%fused_computation.2 | loop fusion | flops 12582912 | bytes 17825792 | tf_op jit(solution)/shard_map/sub | solution.py:70
  501.7 28.5 %fusion = bf16[1024,64,128]{2,1,0:T(8,128)(2,1)} fusion(f32[1024,64,64]{2,1,0:T(8,128)} %multiply_subtract_fusion, f32[1024,64,64]{2,1,0:T(8,128)} %fusion.117), kind=kLoop, calls=%fused_computation.1 | loop fusion | flops 25165824 | bytes 50331648 | tf_op jit(solution)/shard_map/convert_element_type | solution.py:75
  530.1 14.8 %reshape.411 = bf16[512,32,2,64]{3,2,1,0:T(2,128)(2,1)} reshape(bf16[16384,128]{1,0:T(8,128)(2,1)} %all-gather.5.cloned.1.call-done) | data formatting | bytes 8388608 | tf_op jit(solution)/shard_map/reshape | solution.py:180
  544.9 15.5 %copy.136 = bf16[512,32,2,64]{0,1,2,3:T(8,128)(2,1)} copy(bf16[512,32,2,64]{3,2,1,0:T(2,128)(2,1)} %reshape.411) | data formatting | bytes 8388608 | tf_op jit(solution)/shard_map/reshape | solution.py:180
  560.4 2.9 fusion.38
  564.1 2.3 copy.140
  566.5 7.9 %fusion.10 = bf16[64,2,64,128]{3,2,1,0:T(8,128)(2,1)} fusion(f32[2,64,128,64]{2,3,1,0:T(8,128)} %fusion.16, bf16[64,2,64,32]{2,3,1,0:T(8,128)(2,1)} %bitcast.234, bf16[16,128]{1,0:T(8,128)(2,1)S(1)} %get-tuple-element.31, bf16[16,128]{1,0:T(8,128)(2,1)S(1)} %get-tuple-element.32), kind=kOutput, calls=%fused_computation.15 | convolution fusion | flops 69222400 | bytes 6823936 | tf_op jit(solution)/shard_map/dot_general | solution.py:198
  (67 shorter events, 24.6 us)
Async XLA Ops:
  7.2 1.6 copy-start
  7.2 150.4 %reduce-scatter.3.cloned.1.call-start = ((), (), s32[]{:S(2)}) async-start(), calls=%async_computation.2 | async-start | bytes 8912896 | tf_op jit(solution)/shard_map/reduce_scatter | solution.py:115
  7.7 4.7 copy-start.4
  7.7 4.7 copy-start.6
  50.1 172.7 %all-gather.3.cloned.1.call-start = ((), (), s32[]{:S(2)}) async-start(), calls=%async_computation.3 | async-start | bytes 4456448 | tf_op jit(solution)/shard_map/all_gather | solution.py:125
  168.0 5.0 copy-start.8
  172.3 251.3 %reduce-scatter.5.cloned.1.call-start = ((), (), s32[]{:S(2)}) async-start(), calls=%async_computation.4 | async-start | bytes 8912896 | tf_op jit(solution)/shard_map/reduce_scatter | solution.py:165
  259.2 6.3 %copy-start.9 = (f32[64]{0:T(128)S(1)}, f32[64]{0:T(128)}, u32[]{:S(2)}) copy-start(f32[64]{0:T(128)} %param.9) | copy-start | bytes 772
  320.2 209.9 %all-gather.5.cloned.1.call-start = ((), (), s32[]{:S(2)}) async-start(), calls=%async_computation.5 | async-start | bytes 4456448 | tf_op jit(solution)/shard_map/all_gather | solution.py:177
  442.7 12.4 %copy-start.3 = (f32[1024,1,64]{2,1,0:T(1,128)S(1)}, f32[1024,1,64]{2,1,0:T(1,128)}, u32[]{:S(2)}) copy-start(f32[1024,1,64]{2,1,0:T(1,128)} %fusion.115) | copy-start | bytes 786436
  466.4 12.5 %copy-start.2 = (f32[1024,64]{1,0:T(8,128)S(1)}, f32[1024,64]{1,0:T(8,128)}, u32[]{:S(2)}) copy-start(f32[1024,64]{1,0:T(8,128)} %copy.148) | copy-start | bytes 786436
  560.4 3.3 copy-start.5
  560.4 3.3 copy-start.7
  564.1 10.3 %copy-start.1 = (bf16[64,2,64,128]{3,2,1,0:T(8,128)(2,1)S(1)}, bf16[64,2,64,128]{3,2,1,0:T(8,128)(2,1)}, u32[]{:S(2)}) copy-start(bf16[64,2,64,128]{3,2,1,0:T(8,128)(2,1)} %param.5) | copy-start | bytes 6291460
Sparse Core Ops, SparseCore 0:
  50.2 107.2 reduce-scatter.2
  172.4 50.3 all-gather.2
  320.3 103.1 reduce-scatter.4
  456.2 50.4 all-gather.4
where the time goes:
time: 591 us; the launch traced here: 581 us
  waiting for transfers between devices  257 us (43%)
  local copies, waits for them, and re-layouts  153 us (26%)
  matrix products  96.8 us (16%)
  other arithmetic  59.4 us (10%)
  between operations  14.5 us (2%)
    reduce_scatter x1, waiting for transfers between devices, body(): lax.psum_scatter(jnp.einsum('cxaq,xabk->qkbc', section, across_local, pre...  107 us
    reduce_scatter x1, waiting for transfers between devices, body(): lax.psum_scatter(jnp.einsum('oxbq,kabx->qkao', section, back_local, prefe...  103 us
    all_gather x1, waiting for transfers between devices, body(): every_mode = lax.all_gather(spectral, 'gx', axis=0, tiled=True)  46.1 us
    reshape x2, local copies, waits for them, and re-layouts, body(): every_grad.reshape(wave_pairs, MX, 2, channels)  30.3 us
    reshape x2, local copies, waits for them, and re-layouts, body(): every_mode.reshape(wave_pairs, MX, 2, channels)  30 us
    convert_element_type x1, other arithmetic, mode_grads(): (jnp.concatenate([real_w, imag_w], 2) * weight_scale).astype(jnp.bfloat16)  28.5 us
    sub x1, other arithmetic, mode_grads(): jnp.einsum('mc,mo->mco', stacked[:, 0], grad_pairs[:, 1], preferred_eleme...  22.8 us
    reshape x1, local copies, waits for them, and re-layouts, body(): mode_sums = lax.psum_scatter(jnp.einsum('cxaq,xabk->qkbc', section, acros...  16.4 us
  transfers between devices with their start and end apart: 4, of which 3 were waited for; matrix products, arithmetic and copies ran while one was open for 13% of the time, Pallas kernels for 0%

commit v1 on v0

--- a/solution.py
+++ b/solution.py
@@ -122,7 +122,16 @@
     )
     coeffs = (mode_sums * forward_scale).astype(jnp.bfloat16)
     spectral = mode_product(coeffs, spectral_weight, channels)
-    every_mode = lax.all_gather(spectral, "gx", axis=0, tiled=True)
+    ways = lax.axis_size("gx")
+    up = [(d, (d + 1) % ways) for d in range(ways)]
+    down = [(d, (d - 1) % ways) for d in range(ways)]
+    earlier, later = ([spectral], [spectral])
+    for _ in range(ways // 2):
+        earlier.append(lax.ppermute(earlier[-1], "gx", up))
+    for _ in range((ways - 1) // 2):
+        later.append(lax.ppermute(later[-1], "gx", down))
+    line = jnp.concatenate([*earlier[::-1], *later[1:]], axis=0)
+    every_mode = jnp.roll(line, (lax.axis_index("gx") - ways // 2) * spectral.shape[0], axis=0)
     planes_back = jnp.einsum(
         "qkao,kabx->oxbq",
         every_mode.reshape(wave_pairs, MX, 2, channels),

time: 591 us -> 638 us (1.080)
  starting transfers between devices: 0.69 us -> 45.4 us
  local copies, waits for them, and re-layouts: 153 us -> 165 us
  waiting for transfers between devices: 257 us -> 245 us
    all_gather x1 -> x0, waiting for transfers between devices: 46.1 us -> none  [body(): every_mode = lax.all_gather(spectral, 'gx', axis=0, tiled=True)]
    ppermute x0 -> x15, starting transfers between devices: none -> 45.3 us  [the longest x7 45.2 us: body(): later.append(lax.ppermute(later[-1], 'gx', down))]
    ppermute x0 -> x15, waiting for transfers between devices: none -> 31.7 us  [the longest x8 29 us: body(): earlier.append(lax.ppermute(earlier[-1], 'gx', up))]
    unnamed x20 -> x69, local copies, waits for them, and re-layouts: 1.14 us -> 10.1 us
    dynamic_slice x0 -> x2, local copies, waits for them, and re-layouts: none -> 8.74 us  [body(): jnp.roll(line, (lax.axis_index('gx') - ways // 2) * spectral.shape[0], ax...]
    all_gather x1 -> x0, local copies, waits for them, and re-layouts: 6.41 us -> none  [body(): every_mode = lax.all_gather(spectral, 'gx', axis=0, tiled=True)]
  transfers between devices with their start and end apart: 4 -> 18, of which waited for: 3 -> 13; matrix products, arithmetic and copies ran while one was open for 13% -> 13% of each run, Pallas kernels for 0% -> 0%
where the time goes in v1:
time: 638 us; the launch traced here: 626 us
  waiting for transfers between devices  245 us (38%)
  local copies, waits for them, and re-layouts  165 us (26%)
  matrix products  97.9 us (15%)
  other arithmetic  58.7 us (9%)
  starting transfers between devices  45.4 us (7%)
  between operations  14.6 us (2%)
    reduce_scatter x1, waiting for transfers between devices, body(): lax.psum_scatter(jnp.einsum('cxaq,xabk->qkbc', section, across_local, pre...  107 us
    reduce_scatter x1, waiting for transfers between devices, body(): lax.psum_scatter(jnp.einsum('oxbq,kabx->qkao', section, back_local, prefe...  106 us
    ppermute x7, starting transfers between devices, body(): later.append(lax.ppermute(later[-1], 'gx', down))  45.2 us
    reshape x2, local copies, waits for them, and re-layouts, body(): every_grad.reshape(wave_pairs, MX, 2, channels)  30.4 us
    reshape x2, local copies, waits for them, and re-layouts, body(): every_mode.reshape(wave_pairs, MX, 2, channels)  30 us
    ppermute x8, waiting for transfers between devices, body(): earlier.append(lax.ppermute(earlier[-1], 'gx', up))  29 us
    convert_element_type x1, other arithmetic, mode_grads(): (jnp.concatenate([real_w, imag_w], 2) * weight_scale).astype(jnp.bfloat16)  28.4 us
    sub x1, other arithmetic, mode_grads(): jnp.einsum('mc,mo->mco', stacked[:, 0], grad_pairs[:, 1], preferred_eleme...  22.8 us
  transfers between devices with their start and end apart: 18, of which 13 were waited for; matrix products, arithmetic and copies ran while one was open for 13% of the time, Pallas kernels for 0%

profile of v1, /device:TPU:0, one launch (start us, length us, event | category | flops | bytes accessed | tf_op | source)
XLA Modules:
  0.0 626.2 jit_solution(8137123711990404314)
XLA Ops:
  12.7 4.8 convolution_bitcast_fusion.1
  17.5 16.1 %copy.115 = f32[512,32,2,64]{3,2,1,0:T(2,128)} copy(f32[512,32,2,64]{0,1,3,2:T(8,128)} %convolution_bitcast_fusion.1) | data formatting | bytes 16777216 | tf_op jit(solution)/shard_map/cxaq,xabk->qkbc/transpose | solution.py:116
  33.7 16.4 %reshape.402 = f32[16384,128]{1,0:T(8,128)} reshape(f32[512,32,2,64]{3,2,1,0:T(2,128)} %copy.115) | data formatting | bytes 16777216 | tf_op jit(solution)/shard_map/reshape | solution.py:118
  50.1 107.4 %reduce-scatter.3.cloned.1.call-done = f32[1024,128]{1,0:T(8,128)} async-done(((f32[16384,128]{1,0:T(8,128)}), f32[1024,128]{1,0:T(8,128)}) %reduce-scatter.3.cloned.1.call-update) | async-done | bytes 524304 | tf_op jit(solution)/shard_map/reduce_scatter | solution.py:115
  159.2 8.9 %fusion.114 = f32[1024,2,128]{2,1,0:T(2,128)} fusion(bf16[1024,2,64]{2,1,0:T(2,128)(2,1)S(1)} %copy.117, bf16[1024,64,128]{2,1,0:T(8,128)(2,1)} %param.7), kind=kOutput, calls=%fused_computation.196 | convolution fusion | flops 33554432 | bytes 18087936 | tf_op jit(solution)/shard_map/mac,mcj->amj/dot_general | solution.py:59
  171.6 8.5 %collective-permute-done = bf16[1024,128]{0,1:T(8,128)(2,1)S(1)} collective-permute-done((bf16[1024,128]{0,1:T(8,128)(2,1)S(1)}, bf16[1024,128]{0,1:T(8,128)(2,1)S(1)}, u32[]{:S(2)}, u32[]{:S(2)}) %collective-permute-start) | collective-permute-done | bytes 262176 | tf_op jit(solution)/shard_map/ppermute | solution.py:130
  180.1 4.4 collective-permute-start.8
  184.5 4.1 collective-permute-done.1
  189.3 4.5 collective-permute-start.9
  197.7 4.7 collective-permute-start.10
  206.4 4.8 collective-permute-start.11
  215.4 4.7 collective-permute-start.12
  224.3 4.6 collective-permute-start.13
  232.1 3.7 fusion.18
  235.8 17.4 %collective-permute-start.14 = (bf16[1024,128]{0,1:T(8,128)(2,1)S(1)}, bf16[1024,128]{0,1:T(8,128)(2,1)S(1)}, u32[]{:S(2)}, u32[]{:S(2)}) collective-permute-start(bf16[1024,128]{0,1:T(8,128)(2,1)S(1)} %collective-permute-done.13), channel_id=1, source_target_pairs={{0,15},{1,0},{2,1},{3,2},{4,3},{5,4},{6,5},{7,6},{8,7},{9,8},{10,9... | collective-permute-start | bytes 786440 | tf_op jit(solution)/shard_map/ppermute | solution.py:132
  264.0 6.4 %copy.119 = bf16[16384,128]{1,0:T(8,128)(2,1)} copy(bf16[16384,128]{0,1:T(8,128)(2,1)} %constant_dynamic-slice_fusion) | data formatting | bytes 8388608 | tf_op jit(solution)/shard_map/jit(_roll_dynamic)/dynamic_slice | solution.py:134
  270.4 14.7 %reshape.404 = bf16[512,32,2,64]{3,2,1,0:T(2,128)(2,1)} reshape(bf16[16384,128]{1,0:T(8,128)(2,1)} %copy.119) | data formatting | bytes 8388608 | tf_op jit(solution)/shard_map/reshape | solution.py:137
  285.1 15.3 %copy.121 = bf16[512,32,2,64]{0,1,2,3:T(8,128)(2,1)} copy(bf16[512,32,2,64]{3,2,1,0:T(2,128)(2,1)} %reshape.404) | data formatting | bytes 8388608 | tf_op jit(solution)/shard_map/reshape | solution.py:137
  306.5 11.8 %fusion.9 = (bf16[64,2,64,128]{3,2,1,0:T(8,128)(2,1)S(1)}, bf16[64,2,64,128]{3,2,1,0:T(8,128)(2,1)}) fusion(bf16[64,2,64,128]{3,2,1,0:T(8,128)(2,1)} %param.6, f32[64]{0:T(128)S(1)} %copy-done.19, f32[64,2,64,128]{3,0,2,1:T(8,128)} %fusion.18, bf16[64,2,64,32]{2,3,1,0:T(8,128)(2,1)} %bitcast.244, bf16[16,128]{1,0:T(8,128)(2,1)S(1)} %get-tuple-element.31, ...), kind=kOutput, calls=%fused_computation.13 | convolution fusion | flops 93339648 | bytes 11018496 | tf_op jit(solution)/shard_map/dot_general | solution.py:152
  324.1 4.7 convolution_bitcast_fusion
  328.7 16.1 %copy.132 = f32[512,32,2,64]{3,2,1,0:T(2,128)} copy(f32[512,32,2,64]{0,1,3,2:T(8,128)} %convolution_bitcast_fusion) | data formatting | bytes 16777216 | tf_op jit(solution)/shard_map/oxbq,kabx->qkao/transpose | solution.py:175
  344.9 16.4 %reshape.409 = f32[16384,128]{1,0:T(8,128)} reshape(f32[512,32,2,64]{3,2,1,0:T(2,128)} %copy.132) | data formatting | bytes 16777216 | tf_op jit(solution)/shard_map/reshape | solution.py:177
  361.3 105.6 %reduce-scatter.5.cloned.1.call-done = f32[1024,128]{1,0:T(8,128)} async-done(((f32[16384,128]{1,0:T(8,128)}), f32[1024,128]{1,0:T(8,128)}) %reduce-scatter.5.cloned.1.call-update) | async-done | bytes 524304 | tf_op jit(solution)/shard_map/reduce_scatter | solution.py:174
  471.8 13.0 %fusion.115 = f32[1024,1,64]{2,1,0:T(1,128)} fusion(bf16[1024,128,1]{1,2,0:T(2,128)(2,1)} %copy.163, bf16[1024,64,128]{2,1,0:T(8,128)(2,1)} %param.7), kind=kOutput, calls=%fused_computation.197 | convolution fusion | flops 16777216 | bytes 17301504 | tf_op jit(solution)/shard_map/mcj,mj->mc/dot_general | solution.py:78
  485.9 12.4 %fusion.116 = f32[1024,1,64]{2,1,0:T(1,128)S(1)} fusion(bf16[1024,128,1]{1,2,0:T(2,128)(2,1)} %copy.165, bf16[1024,64,128]{2,1,0:T(8,128)(2,1)} %param.7), kind=kOutput, calls=%fused_computation.198 | convolution fusion | flops 16777216 | bytes 17301504 | tf_op jit(solution)/shard_map/mcj,mj->mc/dot_general | solution.py:79
  503.2 3.7 fusion.16
  509.6 12.4 %fusion.117 = f32[1024,64,64]{2,1,0:T(8,128)} fusion(bf16[1024,2,64]{2,1,0:T(2,128)(2,1)S(1)} %copy.117, bf16[1024,2,64]{2,1,0:T(2,128)(2,1)S(1)} %copy.144), kind=kOutput, calls=%fused_computation.199 | convolution fusion | flops 16777216 | bytes 17301504 | tf_op jit(solution)/shard_map/mac,mao->mco/dot_general | solution.py:69
  522.0 22.8 %multiply_subtract_fusion = f32[1024,64,64]{2,1,0:T(8,128)} fusion(f32[1024,64]{1,0:T(8,128)S(1)} %copy.148, f32[1024,64]{1,0:T(8,128)S(1)} %copy-done.2, f32[1024,64]{1,0:T(8,128)S(1)} %copy.146, f32[1024,64]{1,0:T(8,128)S(1)} %copy.145), kind=kLoop, calls=%fused_computation.2 | loop fusion | flops 12582912 | bytes 17825792 | tf_op jit(solution)/shard_map/sub | solution.py:70
  544.8 28.4 %fusion = bf16[1024,64,128]{2,1,0:T(8,128)(2,1)} fusion(f32[1024,64,64]{2,1,0:T(8,128)} %multiply_subtract_fusion, f32[1024,64,64]{2,1,0:T(8,128)} %fusion.117), kind=kLoop, calls=%fused_computation.1 | loop fusion | flops 25165824 | bytes 50331648 | tf_op jit(solution)/shard_map/convert_element_type | solution.py:75
  573.3 14.7 %reshape.411 = bf16[512,32,2,64]{3,2,1,0:T(2,128)(2,1)} reshape(bf16[16384,128]{1,0:T(8,128)(2,1)} %all-gather.2.cloned.1.call-done) | data formatting | bytes 8388608 | tf_op jit(solution)/shard_map/reshape | solution.py:189
  588.0 15.6 %copy.135 = bf16[512,32,2,64]{0,1,2,3:T(8,128)(2,1)} copy(bf16[512,32,2,64]{3,2,1,0:T(2,128)(2,1)} %reshape.411) | data formatting | bytes 8388608 | tf_op jit(solution)/shard_map/reshape | solution.py:189
  611.5 7.9 %fusion.10 = bf16[64,2,64,128]{3,2,1,0:T(8,128)(2,1)} fusion(f32[2,64,128,64]{2,3,1,0:T(8,128)} %fusion.16, bf16[64,2,64,32]{2,3,1,0:T(8,128)(2,1)} %bitcast.234, bf16[16,128]{1,0:T(8,128)(2,1)S(1)} %get-tuple-element.31, bf16[16,128]{1,0:T(8,128)(2,1)S(1)} %get-tuple-element.32), kind=kOutput, calls=%fused_computation.15 | convolution fusion | flops 69222400 | bytes 6823936 | tf_op jit(solution)/shard_map/dot_general | solution.py:207
  (147 shorter events, 74.6 us)
Async XLA Ops:
  7.2 150.3 %reduce-scatter.3.cloned.1.call-start = ((), (), s32[]{:S(2)}) async-start(), calls=%async_computation.2 | async-start | bytes 8912896 | tf_op jit(solution)/shard_map/reduce_scatter | solution.py:115
  50.1 416.9 %reduce-scatter.5.cloned.1.call-start = ((), (), s32[]{:S(2)}) async-start(), calls=%async_computation.3 | async-start | bytes 8912896 | tf_op jit(solution)/shard_map/reduce_scatter | solution.py:174
  159.1 73.0 %copy-start.18 = (bf16[64,64]{1,0:T(8,128)(2,1)S(1)}, bf16[64,64]{1,0:T(8,128)(2,1)}, u32[]{:S(2)}) copy-start(bf16[64,64]{1,0:T(8,128)(2,1)} %param.8) | copy-start | bytes 24580
  171.5 8.5 %collective-permute-start = (bf16[1024,128]{0,1:T(8,128)(2,1)S(1)}, bf16[1024,128]{0,1:T(8,128)(2,1)S(1)}, u32[]{:S(2)}, u32[]{:S(2)}) collective-permute-start(bf16[1024,128]{0,1:T(8,128)(2,1)S(1)} %pad_maximum_fusion), channel_id=1, source_target_pairs={{0,1},{1,2},{2,3},{3,4},{4,5},{5,6},{6,7},{7,8},{8,9},{9,10},{10,1... | collective-permute-start | bytes 786440 | tf_op jit(solution)/shard_map/ppermute | solution.py:130
  180.1 8.5 %collective-permute-start.1 = (bf16[1024,128]{0,1:T(8,128)(2,1)S(1)}, bf16[1024,128]{0,1:T(8,128)(2,1)S(1)}, u32[]{:S(2)}, u32[]{:S(2)}) collective-permute-start(bf16[1024,128]{0,1:T(8,128)(2,1)S(1)} %collective-permute-done), channel_id=1, source_target_pairs={{0,1},{1,2},{2,3},{3,4},{4,5},{5,6},{6,7},{7,8},{8,9},{9,10},{10,1... | collective-permute-start | bytes 786440 | tf_op jit(solution)/shard_map/ppermute | solution.py:130
  180.1 8.5 %collective-permute-start.8 = (bf16[1024,128]{0,1:T(8,128)(2,1)S(1)}, bf16[1024,128]{0,1:T(8,128)(2,1)S(1)}, u32[]{:S(2)}, u32[]{:S(2)}) collective-permute-start(bf16[1024,128]{0,1:T(8,128)(2,1)S(1)} %pad_maximum_fusion), channel_id=1, source_target_pairs={{0,15},{1,0},{2,1},{3,2},{4,3},{5,4},{6,5},{7,6},{8,7},{9,8},{10,9... | collective-permute-start | bytes 786440 | tf_op jit(solution)/shard_map/ppermute | solution.py:132
  188.6 9.2 %copy-start.5 = (bf16[1024,128]{0,1:T(8,128)(2,1)}, bf16[1024,128]{0,1:T(8,128)(2,1)S(1)}, u32[]{:S(2)}) copy-start(bf16[1024,128]{0,1:T(8,128)(2,1)S(1)} %collective-permute-done.1) | copy-start | bytes 786436
  188.6 8.6 %collective-permute-start.2 = (bf16[1024,128]{0,1:T(8,128)(2,1)S(1)}, bf16[1024,128]{0,1:T(8,128)(2,1)S(1)}, u32[]{:S(2)}, u32[]{:S(2)}) collective-permute-start(bf16[1024,128]{0,1:T(8,128)(2,1)S(1)} %collective-permute-done.1), channel_id=1, source_target_pairs={{0,1},{1,2},{2,3},{3,4},{4,5},{5,6},{6,7},{7,8},{8,9},{9,10},{10,1... | collective-permute-start | bytes 786440 | tf_op jit(solution)/shard_map/ppermute | solution.py:130
  189.3 8.4 %collective-permute-start.9 = (bf16[1024,128]{0,1:T(8,128)(2,1)S(1)}, bf16[1024,128]{0,1:T(8,128)(2,1)S(1)}, u32[]{:S(2)}, u32[]{:S(2)}) collective-permute-start(bf16[1024,128]{0,1:T(8,128)(2,1)S(1)} %collective-permute-done.8), channel_id=1, source_target_pairs={{0,15},{1,0},{2,1},{3,2},{4,3},{5,4},{6,5},{7,6},{8,7},{9,8},{10,9... | collective-permute-start | bytes 786440 | tf_op jit(solution)/shard_map/ppermute | solution.py:132
  197.2 9.2 %copy-start.9 = (bf16[1024,128]{0,1:T(8,128)(2,1)}, bf16[1024,128]{0,1:T(8,128)(2,1)S(1)}, u32[]{:S(2)}) copy-start(bf16[1024,128]{0,1:T(8,128)(2,1)S(1)} %collective-permute-done.2) | copy-start | bytes 786436
  197.2 8.6 %collective-permute-start.3 = (bf16[1024,128]{0,1:T(8,128)(2,1)S(1)}, bf16[1024,128]{0,1:T(8,128)(2,1)S(1)}, u32[]{:S(2)}, u32[]{:S(2)}) collective-permute-start(bf16[1024,128]{0,1:T(8,128)(2,1)S(1)} %collective-permute-done.2), channel_id=1, source_target_pairs={{0,1},{1,2},{2,3},{3,4},{4,5},{5,6},{6,7},{7,8},{8,9},{9,10},{10,1... | collective-permute-start | bytes 786440 | tf_op jit(solution)/shard_map/ppermute | solution.py:130
  197.7 8.6 %collective-permute-start.10 = (bf16[1024,128]{0,1:T(8,128)(2,1)S(1)}, bf16[1024,128]{0,1:T(8,128)(2,1)}, u32[]{:S(2)}, u32[]{:S(2)}) collective-permute-start(bf16[1024,128]{0,1:T(8,128)(2,1)S(1)} %collective-permute-done.9), channel_id=1, source_target_pairs={{0,15},{1,0},{2,1},{3,2},{4,3},{5,4},{6,5},{7,6},{8,7},{9,8},{10,9... | collective-permute-start | bytes 786440 | tf_op jit(solution)/shard_map/ppermute | solution.py:132
  205.8 8.7 %collective-permute-start.4 = (bf16[1024,128]{0,1:T(8,128)(2,1)S(1)}, bf16[1024,128]{0,1:T(8,128)(2,1)}, u32[]{:S(2)}, u32[]{:S(2)}) collective-permute-start(bf16[1024,128]{0,1:T(8,128)(2,1)S(1)} %collective-permute-done.3), channel_id=1, source_target_pairs={{0,1},{1,2},{2,3},{3,4},{4,5},{5,6},{6,7},{7,8},{8,9},{9,10},{10,1... | collective-permute-start | bytes 786440 | tf_op jit(solution)/shard_map/ppermute | solution.py:130
  206.4 9.0 %collective-permute-start.11 = (bf16[1024,128]{0,1:T(8,128)(2,1)}, bf16[1024,128]{0,1:T(8,128)(2,1)}, u32[]{:S(2)}, u32[]{:S(2)}) collective-permute-start(bf16[1024,128]{0,1:T(8,128)(2,1)} %collective-permute-done.10), channel_id=1, source_target_pairs={{0,15},{1,0},{2,1},{3,2},{4,3},{5,4},{6,5},{7,6},{8,7},{9,8},{10,9... | collective-permute-start | bytes 786440 | tf_op jit(solution)/shard_map/ppermute | solution.py:132
  214.5 8.9 %collective-permute-start.5 = (bf16[1024,128]{0,1:T(8,128)(2,1)}, bf16[1024,128]{0,1:T(8,128)(2,1)}, u32[]{:S(2)}, u32[]{:S(2)}) collective-permute-start(bf16[1024,128]{0,1:T(8,128)(2,1)} %collective-permute-done.4), channel_id=1, source_target_pairs={{0,1},{1,2},{2,3},{3,4},{4,5},{5,6},{6,7},{7,8},{8,9},{9,10},{10,1... | collective-permute-start | bytes 786440 | tf_op jit(solution)/shard_map/ppermute | solution.py:130
  214.5 40.7 %copy-start.12 = (bf16[1024,128]{0,1:T(8,128)(2,1)S(1)}, bf16[1024,128]{0,1:T(8,128)(2,1)}, u32[]{:S(2)}) copy-start(bf16[1024,128]{0,1:T(8,128)(2,1)} %copy-done.11) | copy-start | bytes 786436
  214.5 40.8 %copy-start.10 = (bf16[1024,128]{0,1:T(8,128)(2,1)S(1)}, bf16[1024,128]{0,1:T(8,128)(2,1)}, u32[]{:S(2)}) copy-start(bf16[1024,128]{0,1:T(8,128)(2,1)} %copy-done.9) | copy-start | bytes 786436
  214.5 40.8 %copy-start.6 = (bf16[1024,128]{0,1:T(8,128)(2,1)S(1)}, bf16[1024,128]{0,1:T(8,128)(2,1)}, u32[]{:S(2)}) copy-start(bf16[1024,128]{0,1:T(8,128)(2,1)} %copy-done.5) | copy-start | bytes 786436
  214.5 40.9 %copy-start.4 = (bf16[1024,128]{0,1:T(8,128)(2,1)S(1)}, bf16[1024,128]{0,1:T(8,128)(2,1)}, u32[]{:S(2)}) copy-start(bf16[1024,128]{0,1:T(8,128)(2,1)} %copy-done.3) | copy-start | bytes 786436
  214.5 40.9 %copy-start.8 = (bf16[1024,128]{0,1:T(8,128)(2,1)S(1)}, bf16[1024,128]{0,1:T(8,128)(2,1)}, u32[]{:S(2)}) copy-start(bf16[1024,128]{0,1:T(8,128)(2,1)} %copy-done.7) | copy-start | bytes 786436
  215.4 8.9 %collective-permute-start.12 = (bf16[1024,128]{0,1:T(8,128)(2,1)}, bf16[1024,128]{0,1:T(8,128)(2,1)S(1)}, u32[]{:S(2)}, u32[]{:S(2)}) collective-permute-start(bf16[1024,128]{0,1:T(8,128)(2,1)} %collective-permute-done.11), channel_id=1, source_target_pairs={{0,15},{1,0},{2,1},{3,2},{4,3},{5,4},{6,5},{7,6},{8,7},{9,8},{10,9... | collective-permute-start | bytes 786440 | tf_op jit(solution)/shard_map/ppermute | solution.py:132
  223.4 8.7 %collective-permute-start.6 = (bf16[1024,128]{0,1:T(8,128)(2,1)}, bf16[1024,128]{0,1:T(8,128)(2,1)S(1)}, u32[]{:S(2)}, u32[]{:S(2)}) collective-permute-start(bf16[1024,128]{0,1:T(8,128)(2,1)} %collective-permute-done.5), channel_id=1, source_target_pairs={{0,1},{1,2},{2,3},{3,4},{4,5},{5,6},{6,7},{7,8},{8,9},{9,10},{10,1... | collective-permute-start | bytes 786440 | tf_op jit(solution)/shard_map/ppermute | solution.py:130
  224.3 11.5 %collective-permute-start.13 = (bf16[1024,128]{0,1:T(8,128)(2,1)S(1)}, bf16[1024,128]{0,1:T(8,128)(2,1)S(1)}, u32[]{:S(2)}, u32[]{:S(2)}) collective-permute-start(bf16[1024,128]{0,1:T(8,128)(2,1)S(1)} %collective-permute-done.12), channel_id=1, source_target_pairs={{0,15},{1,0},{2,1},{3,2},{4,3},{5,4},{6,5},{7,6},{8,7},{9,8},{10,9... | collective-permute-start | bytes 786440 | tf_op jit(solution)/shard_map/ppermute | solution.py:132
  232.1 21.1 %collective-permute-start.7 = (bf16[1024,128]{0,1:T(8,128)(2,1)S(1)}, bf16[1024,128]{0,1:T(8,128)(2,1)S(1)}, u32[]{:S(2)}, u32[]{:S(2)}) collective-permute-start(bf16[1024,128]{0,1:T(8,128)(2,1)S(1)} %collective-permute-done.6), channel_id=1, source_target_pairs={{0,1},{1,2},{2,3},{3,4},{4,5},{5,6},{6,7},{7,8},{8,9},{9,10},{10,1... | collective-permute-start | bytes 786440 | tf_op jit(solution)/shard_map/ppermute | solution.py:130
  235.8 21.7 %collective-permute-start.14 = (bf16[1024,128]{0,1:T(8,128)(2,1)S(1)}, bf16[1024,128]{0,1:T(8,128)(2,1)S(1)}, u32[]{:S(2)}, u32[]{:S(2)}) collective-permute-start(bf16[1024,128]{0,1:T(8,128)(2,1)S(1)} %collective-permute-done.13), channel_id=1, source_target_pairs={{0,15},{1,0},{2,1},{3,2},{4,3},{5,4},{6,5},{7,6},{8,7},{9,8},{10,9... | collective-permute-start | bytes 786440 | tf_op jit(solution)/shard_map/ppermute | solution.py:132
  285.1 21.4 %copy-start.19 = (f32[64]{0:T(128)S(1)}, f32[64]{0:T(128)}, u32[]{:S(2)}) copy-start(f32[64]{0:T(128)} %param.9) | copy-start | bytes 772
  361.3 212.0 %all-gather.2.cloned.1.call-start = ((), (), s32[]{:S(2)}) async-start(), calls=%async_computation.4 | async-start | bytes 4456448 | tf_op jit(solution)/shard_map/all_gather | solution.py:186
  485.9 12.4 %copy-start.13 = (f32[1024,1,64]{2,1,0:T(1,128)S(1)}, f32[1024,1,64]{2,1,0:T(1,128)}, u32[]{:S(2)}) copy-start(f32[1024,1,64]{2,1,0:T(1,128)} %fusion.115) | copy-start | bytes 786436
  509.6 12.5 %copy-start.2 = (f32[1024,64]{1,0:T(8,128)S(1)}, f32[1024,64]{1,0:T(8,128)}, u32[]{:S(2)}) copy-start(f32[1024,64]{1,0:T(8,128)} %copy.147) | copy-start | bytes 786436
  588.0 19.6 %copy-start.15 = (bf16[64,1,2,32]{0,3,1,2:T(8,128)(2,1)S(1)}, bf16[64,1,2,32]{0,3,1,2:T(8,128)(2,1)}, u32[]{:S(2)}) copy-start(bf16[64,1,2,32]{0,3,1,2:T(8,128)(2,1)} %copy-done.14) | copy-start | bytes 24580
  588.0 19.6 %copy-start.17 = (bf16[64,1,2,32]{0,3,1,2:T(8,128)(2,1)S(1)}, bf16[64,1,2,32]{0,3,1,2:T(8,128)(2,1)}, u32[]{:S(2)}) copy-start(bf16[64,1,2,32]{0,3,1,2:T(8,128)(2,1)} %copy-done.16) | copy-start | bytes 24580
  588.0 31.4 %copy-start.1 = (bf16[64,2,64,128]{3,2,1,0:T(8,128)(2,1)S(1)}, bf16[64,2,64,128]{3,2,1,0:T(8,128)(2,1)}, u32[]{:S(2)}) copy-start(bf16[64,2,64,128]{3,2,1,0:T(8,128)(2,1)} %param.5) | copy-start | bytes 6291460
  (6 other events, 22.0 us)
Sparse Core Ops, SparseCore 0:
  50.2 107.2 reduce-scatter.2
  361.4 105.4 reduce-scatter.4
  499.3 50.2 all-gather.1
